TPU v7x, 32 devices: a whole 2x2x4 slice. The times are simulated.
32 devices in a mesh: tier: 2 (over x), row: 16 (over z, y, core).
Axes of the slice: x: 2, y: 2, z: 4, core: 2. Of those that a mesh axis runs over, the one named last changes fastest.
Arguments:
- current_modes: float32 [8192, 128], P(('tier', 'row')), may hold values from -6 to 6
- previous: float32 [8192, 128], P(('tier', 'row')), may hold values from -4 to 4
- diag_tiles: bfloat16 [2, 16, 2, 128, 128], P('tier', 'row'), may hold values from -2 to 8, as said below
- lateral_tiles: bfloat16 [2, 16, 2, 2, 128, 128], P('tier', 'row'), may hold values from -0.25 to 0.25
- lateral_index: int32 [2, 16, 2, 2], P('tier', 'row'), may hold values from 0 to 3, as said below
- vertical_tiles: bfloat16 [2, 16, 2, 128, 128], P('tier', 'row'), may hold values from -0.5 to 0.5
- vertical_index: int32 [2, 16, 2], P('tier', 'row'), may hold values from 0 to 1, each once within a row
- smoother: float32 [2, 16, 2, 128, 128], P('tier', 'row'), may hold values from -1 to 2
Outputs:
- ortho_basis: float32 [8192, 384], P(('tier', 'row'))
- projected: float32 [384, 384], replicated
Inputs may be any that keep to these rules, and one draw needn't show every extreme that they name: lateral_index[t,r,g,0] lies in 0 to g and lateral_index[t,r,g,1] in g+2 to 3; slot 0 is the last tile of the previous row block, slots 1 to 2 this block's tiles, slot 3 the first tile of the next row block. `vertical_index`: the entries of one row block form a permutation of its tiles. `diag_tiles`: each tile is symmetric.
All inputs are finite; a program needn't handle non-finite values.
Results may differ from a plain program's by a relative error of at most 0.0015.
The roundings to bfloat16 on the way count: a program that leaves them out, or rounds other values in their place, can miss the bound.
Values may be sent and summed in bfloat16 or wider, within the bound.
A program may use at most 64 MiB of HBM per device.

v0:
```python
import jax
import jax.numpy as jnp
from jax import lax
from jax.sharding import PartitionSpec as P


def with_halo(x, sides, width):
    for axis, dim in sides:
        devices, length = (lax.axis_size(axis), x.shape[dim])
        up = [(i, (i + 1) % devices) for i in range(devices - 1)]
        down = [(j, i) for i, j in up]
        last = lax.slice_in_dim(x, length - width, length, axis=dim)
        first = lax.slice_in_dim(x, 0, width, axis=dim)
        before = lax.ppermute(last, axis, up)
        after = lax.ppermute(first, axis, down)
        x = jnp.concatenate([before, x, after], axis=dim)
    return x


def shifted(value, axis, steps):
    count = lax.axis_size(axis)
    first, last = (max(0, -steps), min(count, count - steps))
    return lax.ppermute(value, axis, [(source, source + steps) for source in range(first, last)])


def apply_operator(
    values, diag_part, side_part, side_slots, down_part, down_slots, up_part, up_slots
):
    row_count, column_count = values.shape
    tile_count, tile_width = (diag_part.shape[0], diag_part.shape[-1])
    own_tiles = values.reshape(tile_count, tile_width, column_count)
    result = jnp.einsum("jik,jkc->jic", diag_part, own_tiles, preferred_element_type=jnp.float32)
    framed = with_halo(values, (("row", 0),), tile_width).reshape(
        tile_count + 2, tile_width, column_count
    )
    result = result + jnp.einsum(
        "jbik,jbkc->jic", side_part, framed[side_slots], preferred_element_type=jnp.float32
    )
    mirror = jnp.einsum("jbki,jkc->jbic", side_part, own_tiles, preferred_element_type=jnp.float32)
    onehot = (
        side_slots[:, :, None] == jnp.arange(tile_count + 2, dtype=jnp.int32)[None, None, :]
    ).astype(jnp.float32)
    spread = jnp.einsum("jbs,jbic->sic", onehot, mirror, precision=lax.Precision.HIGHEST)
    from_next = shifted(spread[0].astype(jnp.bfloat16), "row", -1).astype(jnp.float32)
    from_prev = shifted(spread[tile_count + 1].astype(jnp.bfloat16), "row", 1).astype(jnp.float32)
    result = result + spread[1 : tile_count + 1]
    result = result.at[tile_count - 1].add(from_next).at[0].add(from_prev)
    layers = with_halo(values, (("tier", 0),), row_count)
    lower_layer = layers[:row_count].reshape(tile_count, tile_width, column_count)
    upper_layer = layers[2 * row_count :].reshape(tile_count, tile_width, column_count)
    result = result + jnp.einsum(
        "jik,jkc->jic", down_part, lower_layer[down_slots], preferred_element_type=jnp.float32
    )
    lifted = jnp.einsum("kij,kic->kjc", up_part, upper_layer, preferred_element_type=jnp.float32)
    placing = (up_slots[:, None] == jnp.arange(tile_count, dtype=jnp.int32)[None, :]).astype(
        jnp.float32
    )
    result = result + jnp.einsum("kj,kic->jic", placing, lifted, precision=lax.Precision.HIGHEST)
    return result.reshape(row_count, column_count)


def gram_of(left_side, right_side):
    return jnp.dot(left_side.T, right_side, precision=lax.Precision.HIGHEST)


def lower_solve(factor, matrix):
    return jax.scipy.linalg.solve_triangular(factor, matrix.T, lower=True).T


def on_device(
    current_modes,
    previous,
    diag_tiles,
    lateral_tiles,
    lateral_index,
    vertical_tiles,
    vertical_index,
    smoother,
):
    highest = lax.Precision.HIGHEST
    diag_part = diag_tiles[0, 0]
    side_part = lateral_tiles[0, 0]
    side_slots = lateral_index[0, 0]
    down_part = vertical_tiles[0, 0]
    down_slots = vertical_index[0, 0]
    relax_part = smoother[0, 0]
    up_part, up_slots = shifted((down_part, down_slots), "tier", -1)
    row_count, mode_count = current_modes.shape
    tile_count, tile_width = (relax_part.shape[0], relax_part.shape[-1])

    def operate(values):
        return apply_operator(
            values, diag_part, side_part, side_slots, down_part, down_slots, up_part, up_slots
        )

    paired = operate(jnp.concatenate([current_modes, previous], 1).astype(jnp.bfloat16))
    mode_image = paired[:, :mode_count]
    prev_image = paired[:, mode_count:]
    along_sum, norm_sum = lax.psum(
        (jnp.sum(current_modes * mode_image, 0), jnp.sum(current_modes * current_modes, 0)),
        ("tier", "row"),
    )
    residue = (mode_image - current_modes * (along_sum / norm_sum)).reshape(
        tile_count, tile_width, mode_count
    )
    coupling = down_part.astype(jnp.float32)

    def relax_tier(lower_field):
        coupled = jnp.einsum("jik,jkc->jic", coupling, lower_field[down_slots], precision=highest)
        return jnp.einsum("jik,jkc->jic", relax_part, residue - coupled, precision=highest)

    def advance(index_value, sweep_field):
        return relax_tier(shifted(sweep_field, "tier", 1))

    sweep_field = lax.fori_loop(
        0, lax.axis_size("tier") - 1, advance, relax_tier(jnp.zeros_like(residue))
    )
    precond = sweep_field.reshape(row_count, mode_count)
    work_image = operate(precond.astype(jnp.bfloat16))
    stacked = jnp.concatenate([current_modes, precond, previous], 1)
    images = jnp.concatenate([mode_image, work_image, prev_image], 1)
    inverse_rows = 1.0 / (row_count * lax.axis_size("tier") * lax.axis_size("row"))
    factor = jnp.linalg.cholesky(
        lax.psum(gram_of(stacked, stacked), ("tier", "row")) * inverse_rows
    )
    ortho_basis = lower_solve(factor, stacked)
    mapped = lower_solve(factor, images)
    projected = lax.psum(gram_of(ortho_basis, mapped), ("tier", "row")) * inverse_rows
    return (ortho_basis, projected)


def solution(mesh):
    placed = (
        P(("tier", "row"), None),
        P(("tier", "row"), None),
        P("tier", "row", None, None, None),
        P("tier", "row", None, None, None, None),
        P("tier", "row", None, None),
        P("tier", "row", None, None, None),
        P("tier", "row", None),
        P("tier", "row", None, None, None),
    )
    return jax.shard_map(
        on_device,
        mesh=mesh,
        in_specs=placed,
        out_specs=(P(("tier", "row"), None), P()),
        check_vma=False,
    )
```

profile of v0, /device:TPU:0, one launch (start us, length us, event | category | flops | bytes accessed | tf_op | source)
XLA Modules:
  0.0 469.8 jit_solution(13690702425288591090)
XLA Ops:
  7.2 1.0 convert.30
  8.2 4.8 %collective-permute-start.4 = (bf16[256,256]{1,0:T(8,128)(2,1)S(1)}, bf16[256,256]{1,0:T(8,128)(2,1)S(1)}, u32[]{:S(2)}, u32[]{:S(2)}) collective-permute-start(bf16[256,256]{1,0:T(8,128)(2,1)S(1)} %pad_maximum_fusion.5), channel_id=1, source_target_pairs={{0,16},{1,17},{2,18},{3,19},{4,20},{5,21},{6,22},{7,23},{8,24},{9,... | collective-permute-start | bytes 393224 | tf_op jit(solution)/shard_map/ppermute | solution.py:14
  13.1 1.3 collective-permute-start.6
  14.4 1.5 collective-permute-start
  15.9 1.3 collective-permute-start.1
  17.8 0.7 copy-done.7
  18.5 1.0 convolution_bitcast_fusion
  19.6 1.3 collective-permute-start.2
  21.1 0.6 copy-done.8
  21.7 0.6 gather_fusion.2
  22.3 5.2 %collective-permute-start.3 = (bf16[128,256]{1,0:T(8,128)(2,1)S(1)}, bf16[128,256]{1,0:T(8,128)(2,1)S(1)}, u32[]{:S(2)}, u32[]{:S(2)}) collective-permute-start(bf16[128,256]{1,0:T(8,128)(2,1)S(1)} %get-tuple-element.103), channel_id=1, source_target_pairs={{0,1},{1,2},{2,3},{3,4},{4,5},{5,6},{6,7},{7,8},{8,9},{9,10},{10,1... | collective-permute-start | bytes 196616 | tf_op jit(solution)/shard_map/ppermute | solution.py:23
  27.6 1.3 collective-permute-start.7
  28.9 0.6 gather_fusion
  29.7 0.6 copy-done.6
  30.5 1.3 collective-permute-start.5
  31.9 0.6 gather_fusion.1
  32.5 1.3 collective-permute-done.7
  34.2 1.8 collective-permute-done.5
  36.0 0.6 fusion.28
  36.8 0.7 copy-done.1
  37.5 41.0 %all-reduce.1 = (f32[128]{0:T(128)S(1)}, f32[128]{0:T(128)S(1)}) all-reduce(f32[128]{0:T(128)S(1)} %get-tuple-element.88, f32[128]{0:T(128)S(1)} %get-tuple-element.87), channel_id=1, replica_groups=mesh['tier'=2,'row'=16] {'tier','row'}, use_global_device_ids=true, to_apply=%region_1.0 | all-reduce | flops 256 | bytes 2048 | tf_op jit(solution)/shard_map/psum | solution.py:99
  78.8 0.7 copy-done.5
  79.5 0.4 convolution_bitcast_fusion.7
  79.9 4.2 collective-permute-start.8
  84.1 2.5 collective-permute-done.8
  86.6 0.6 gather_fusion.3
  87.9 1.3 collective-permute-start.14
  89.2 4.5 collective-permute-start.13
  93.8 1.3 collective-permute-start.10
  95.1 3.0 collective-permute-start.9
  98.3 0.6 convolution_bitcast_fusion.3
  98.9 1.6 fusion.20
  100.6 1.3 collective-permute-start.11
  102.0 3.2 collective-permute-start.12
  105.3 0.6 gather_fusion.4
  106.6 0.6 gather_fusion.5
  107.2 0.4 fusion.41
  107.7 122.6 %all-reduce.5.cloned.1.call-done = f32[384,384]{0,1:T(8,128)} async-done(((f32[384,384]{0,1:T(8,128)}), f32[384,384]{0,1:T(8,128)}) %all-reduce.5.cloned.1.call-update) | async-done | bytes 589840 | tf_op jit(solution)/shard_map/psum | solution.py:124
  230.3 1.1 broadcast_multiply_fusion.1
  231.6 0.8 copy-done.2
  232.5 11.7 %cholesky.77 = f32[128,128]{1,0:T(8,128)S(1)} custom-call(f32[128,128]{1,0:T(8,128)S(1)} %cholesky.192), custom_call_target="Cholesky" | custom-call | tf_op jit(solution)/shard_map/jit(cholesky)/cholesky | solution.py:123
  244.3 9.8 %custom-call.22 = f32[1,128,128]{1,2,0:T(8,128)S(1)} custom-call(f32[1,128,128]{2,1,0:T(8,128)S(1)} %get-tuple-element.117), custom_call_target="InvertDiagBlocksLowerTriangular" | custom-call | tf_op jit(solution)/shard_map/jit(cholesky)/cholesky | solution.py:123
  254.7 11.7 %cholesky.162 = f32[128,128]{1,0:T(8,128)S(1)} custom-call(f32[128,128]{1,0:T(8,128)S(1)} %cholesky.196), custom_call_target="Cholesky" | custom-call | tf_op jit(solution)/shard_map/jit(cholesky)/cholesky | solution.py:123
  266.5 10.0 %custom-call.23 = f32[1,128,128]{1,2,0:T(8,128)S(1)} custom-call(f32[1,128,128]{2,1,0:T(8,128)S(1)} %get-tuple-element.114), custom_call_target="InvertDiagBlocksLowerTriangular" | custom-call | tf_op jit(solution)/shard_map/jit(cholesky)/cholesky | solution.py:123
  276.9 11.7 %cholesky.181 = f32[128,128]{1,0:T(8,128)S(1)} custom-call(f32[128,128]{1,0:T(8,128)S(1)} %convolution_subtract_fusion.5), custom_call_target="Cholesky" | custom-call | tf_op jit(solution)/shard_map/jit(cholesky)/cholesky | solution.py:123
  288.7 0.7 compare_reduce_fusion
  289.4 0.7 compare_reduce_fusion.1
  292.0 6.0 %while.12 = (s32[]{:T(128)}, f32[384,384]{1,0:T(8,128)S(1)}, s32[3,2]{0,1:T(2,128)S(1)}, f32[3,128,128]{2,1,0:T(8,128)S(1)}, s32[]{:T(128)}) while((s32[]{:T(128)}, f32[384,384]{1,0:T(8,128)S(1)}, s32[3,2]{0,1:T(2,128)S(1)}, f32[3,128,128]{2,1,0:T(8,128)S(1)}, s32[]{:T(128)}) %tuple.60), condition=%wide.while_cond.4, body=%wide.while_body.4.sunk | while | flops 2 | bytes 131181 | solution.py:67
  292.1 0.5 fusion.118
  292.7 1.4 bitcast_dynamic-update-slice_fusion.2
  294.1 0.5 fusion.118
  294.7 1.4 bitcast_dynamic-update-slice_fusion.2
  296.1 0.5 fusion.118
  296.7 1.4 bitcast_dynamic-update-slice_fusion.2
  298.1 29.5 %custom-call.25 = f32[3,128,128]{1,2,0:T(8,128)S(1)} custom-call(f32[3,128,128]{2,1,0:T(8,128)S(1)} %get-tuple-element.83), custom_call_target="InvertDiagBlocksLowerTriangular" | custom-call | tf_op jit(solution)/shard_map/jit(_solve_triangular)/triangular_solve | solution.py:67
  327.9 0.4 convolution_subtract_fusion.2
  328.6 0.6 convolution_subtract_fusion
  329.8 0.4 convolution_subtract_fusion.3
  330.5 0.6 convolution_subtract_fusion.1
  331.5 1.6 fusion.12
  333.1 0.9 copy.20
  334.1 126.7 %all-reduce.7.cloned.1.call-done = f32[384,384]{0,1:T(8,128)} async-done(((f32[384,384]{0,1:T(8,128)}), f32[384,384]{0,1:T(8,128)}) %all-reduce.7.cloned.1.call-update) | async-done | bytes 589840 | tf_op jit(solution)/shard_map/psum | solution.py:128
  460.8 1.1 broadcast_multiply_fusion
  461.9 1.1 copy.21
  (100 shorter events, 8.0 us)
Async XLA Ops:
  7.2 10.0 %copy-start = (bf16[1,1,2,2,128,128]{5,4,3,2,1,0:T(8,128)(2,1)S(1)}, bf16[1,1,2,2,128,128]{5,4,3,2,1,0:T(8,128)(2,1)}, u32[]{:S(2)}) copy-start(bf16[1,1,2,2,128,128]{5,4,3,2,1,0:T(8,128)(2,1)} %param.21) | copy-start | bytes 393220
  7.2 1.0 copy-start.3
  7.2 223.1 %all-reduce.5.cloned.1.call-start = ((), (), s32[]{:S(2)}) async-start(), calls=%async_computation | async-start | bytes 1179648 | tf_op jit(solution)/shard_map/psum | solution.py:124
  8.2 23.7 %collective-permute-start.4 = (bf16[256,256]{1,0:T(8,128)(2,1)S(1)}, bf16[256,256]{1,0:T(8,128)(2,1)S(1)}, u32[]{:S(2)}, u32[]{:S(2)}) collective-permute-start(bf16[256,256]{1,0:T(8,128)(2,1)S(1)} %pad_maximum_fusion.5), channel_id=1, source_target_pairs={{0,16},{1,17},{2,18},{3,19},{4,20},{5,21},{6,22},{7,23},{8,24},{9,... | collective-permute-start | bytes 393224 | tf_op jit(solution)/shard_map/ppermute | solution.py:14
  13.1 20.7 %collective-permute-start.6 = (bf16[256,256]{1,0:T(8,128)(2,1)S(1)}, bf16[256,256]{1,0:T(8,128)(2,1)S(1)}, u32[]{:S(2)}, u32[]{:S(2)}) collective-permute-start(bf16[256,256]{1,0:T(8,128)(2,1)S(1)} %pad_maximum_fusion.5), channel_id=1, source_target_pairs={{16,0},{17,1},{18,2},{19,3},{20,4},{21,5},{22,6},{23,7},{24,8},{25... | collective-permute-start | bytes 393224 | tf_op jit(solution)/shard_map/ppermute | solution.py:15
  14.4 7.9 %collective-permute-start = (bf16[128,256]{1,0:T(8,128)(2,1)S(1)}, bf16[128,256]{1,0:T(8,128)(2,1)S(1)}, u32[]{:S(2)}, u32[]{:S(2)}) collective-permute-start(bf16[128,256]{1,0:T(8,128)(2,1)S(1)} %get-tuple-element.107), channel_id=1, source_target_pairs={{0,1},{1,2},{2,3},{3,4},{4,5},{5,6},{6,7},{7,8},{8,9},{9,10},{10,1... | collective-permute-start | bytes 196616 | tf_op jit(solution)/shard_map/ppermute | solution.py:14
  15.9 11.7 %collective-permute-start.1 = (bf16[128,256]{1,0:T(8,128)(2,1)S(1)}, bf16[128,256]{1,0:T(8,128)(2,1)S(1)}, u32[]{:S(2)}, u32[]{:S(2)}) collective-permute-start(bf16[128,256]{1,0:T(8,128)(2,1)S(1)} %get-tuple-element.108), channel_id=1, source_target_pairs={{1,0},{2,1},{3,2},{4,3},{5,4},{6,5},{7,6},{8,7},{9,8},{10,9},{11,1... | collective-permute-start | bytes 196616 | tf_op jit(solution)/shard_map/ppermute | solution.py:15
  17.7 0.7 copy-start.7
  19.6 10.9 %collective-permute-start.2 = (bf16[128,256]{1,0:T(8,128)(2,1)S(1)}, bf16[128,256]{1,0:T(8,128)(2,1)S(1)}, u32[]{:S(2)}, u32[]{:S(2)}) collective-permute-start(bf16[128,256]{1,0:T(8,128)(2,1)S(1)} %get-tuple-element.104), channel_id=1, source_target_pairs={{1,0},{2,1},{3,2},{4,3},{5,4},{6,5},{7,6},{8,7},{9,8},{10,9},{11,1... | collective-permute-start | bytes 196616 | tf_op jit(solution)/shard_map/ppermute | solution.py:23
  21.0 0.7 copy-start.8
  21.7 5.9 %copy-start.4 = (bf16[1,1,2,128,128]{4,3,2,1,0:T(8,128)(2,1)S(1)}, bf16[1,1,2,128,128]{4,3,2,1,0:T(8,128)(2,1)}, u32[]{:S(2)}) copy-start(bf16[1,1,2,128,128]{4,3,2,1,0:T(8,128)(2,1)} %param.23) | copy-start | bytes 196612
  22.3 9.5 %collective-permute-start.3 = (bf16[128,256]{1,0:T(8,128)(2,1)S(1)}, bf16[128,256]{1,0:T(8,128)(2,1)S(1)}, u32[]{:S(2)}, u32[]{:S(2)}) collective-permute-start(bf16[128,256]{1,0:T(8,128)(2,1)S(1)} %get-tuple-element.103), channel_id=1, source_target_pairs={{0,1},{1,2},{2,3},{3,4},{4,5},{5,6},{6,7},{7,8},{8,9},{9,10},{10,1... | collective-permute-start | bytes 196616 | tf_op jit(solution)/shard_map/ppermute | solution.py:23
  27.6 6.2 %collective-permute-start.7 = (bf16[2,128,128]{2,1,0:T(8,128)(2,1)S(1)}, bf16[2,128,128]{2,1,0:T(8,128)(2,1)S(1)}, u32[]{:S(2)}, u32[]{:S(2)}) collective-permute-start(bf16[2,128,128]{2,1,0:T(8,128)(2,1)S(1)} %bitcast.244), channel_id=1, source_target_pairs={{16,0},{17,1},{18,2},{19,3},{20,4},{21,5},{22,6},{23,7},{24,8},{25... | collective-permute-start | bytes 196616 | tf_op jit(solution)/shard_map/ppermute | solution.py:23
  29.5 0.8 copy-start.6
  30.5 5.4 %collective-permute-start.5 = (s32[2]{0:T(128)S(1)}, s32[2]{0:T(128)S(1)}, u32[]{:S(2)}, u32[]{:S(2)}) collective-permute-start(s32[2]{0:T(128)S(1)} %bitcast.253), channel_id=1, source_target_pairs={{16,0},{17,1},{18,2},{19,3},{20,4},{21,5},{22,6},{23,7},{24,8},{25... | collective-permute-start | bytes 32 | tf_op jit(solution)/shard_map/ppermute | solution.py:23
  36.6 0.9 copy-start.1
  78.6 0.9 copy-start.5
  79.9 6.7 %collective-permute-start.8 = (f32[2,128,128]{1,2,0:T(8,128)S(1)}, f32[2,128,128]{1,2,0:T(8,128)S(1)}, u32[]{:S(2)}, u32[]{:S(2)}) collective-permute-start(f32[2,128,128]{1,2,0:T(8,128)S(1)} %convolution_bitcast_fusion.7), channel_id=1, source_target_pairs={{0,16},{1,17},{2,18},{3,19},{4,20},{5,21},{6,22},{7,23},{8,24},{9,... | collective-permute-start | bytes 393224 | tf_op jit(solution)/shard_map/while/body/eval_jaxpr/ppermute | solution.py:23
  87.9 18.3 %collective-permute-start.14 = (bf16[256,128]{1,0:T(8,128)(2,1)S(1)}, bf16[256,128]{1,0:T(8,128)(2,1)S(1)}, u32[]{:S(2)}, u32[]{:S(2)}) collective-permute-start(bf16[256,128]{1,0:T(8,128)(2,1)S(1)} %bitcast_convert_fusion.3), channel_id=1, source_target_pairs={{16,0},{17,1},{18,2},{19,3},{20,4},{21,5},{22,6},{23,7},{24,8},{25... | collective-permute-start | bytes 196616 | tf_op jit(solution)/shard_map/ppermute | solution.py:15
  89.2 17.4 %collective-permute-start.13 = (bf16[256,128]{1,0:T(8,128)(2,1)S(1)}, bf16[256,128]{1,0:T(8,128)(2,1)S(1)}, u32[]{:S(2)}, u32[]{:S(2)}) collective-permute-start(bf16[256,128]{1,0:T(8,128)(2,1)S(1)} %bitcast_convert_fusion.3), channel_id=1, source_target_pairs={{0,16},{1,17},{2,18},{3,19},{4,20},{5,21},{6,22},{7,23},{8,24},{9,... | collective-permute-start | bytes 196616 | tf_op jit(solution)/shard_map/ppermute | solution.py:14
  93.8 8.2 %collective-permute-start.10 = (bf16[128,128]{1,0:T(8,128)(2,1)S(1)}, bf16[128,128]{1,0:T(8,128)(2,1)S(1)}, u32[]{:S(2)}, u32[]{:S(2)}) collective-permute-start(bf16[128,128]{1,0:T(8,128)(2,1)S(1)} %get-tuple-element.110), channel_id=1, source_target_pairs={{1,0},{2,1},{3,2},{4,3},{5,4},{6,5},{7,6},{8,7},{9,8},{10,9},{11,1... | collective-permute-start | bytes 98312 | tf_op jit(solution)/shard_map/ppermute | solution.py:15
  95.1 10.2 %collective-permute-start.9 = (bf16[128,128]{1,0:T(8,128)(2,1)S(1)}, bf16[128,128]{1,0:T(8,128)(2,1)S(1)}, u32[]{:S(2)}, u32[]{:S(2)}) collective-permute-start(bf16[128,128]{1,0:T(8,128)(2,1)S(1)} %get-tuple-element.109), channel_id=1, source_target_pairs={{0,1},{1,2},{2,3},{3,4},{4,5},{5,6},{6,7},{7,8},{8,9},{9,10},{10,1... | collective-permute-start | bytes 98312 | tf_op jit(solution)/shard_map/ppermute | solution.py:14
  100.6 5.6 %collective-permute-start.11 = (bf16[128,128]{1,0:T(8,128)(2,1)S(1)}, bf16[128,128]{1,0:T(8,128)(2,1)S(1)}, u32[]{:S(2)}, u32[]{:S(2)}) collective-permute-start(bf16[128,128]{1,0:T(8,128)(2,1)S(1)} %get-tuple-element.106), channel_id=1, source_target_pairs={{1,0},{2,1},{3,2},{4,3},{5,4},{6,5},{7,6},{8,7},{9,8},{10,9},{11,1... | collective-permute-start | bytes 98312 | tf_op jit(solution)/shard_map/ppermute | solution.py:23
  102.0 358.8 %all-reduce.7.cloned.1.call-start = ((), (), s32[]{:S(2)}) async-start(), calls=%async_computation.1 | async-start | bytes 1179648 | tf_op jit(solution)/shard_map/psum | solution.py:128
  102.0 4.2 collective-permute-start.12
  231.4 1.1 copy-start.2
Sparse Core Ops, SparseCore 0:
  102.1 128.1 all-reduce.4
  333.2 127.4 all-reduce.6
where the time goes:
time: 471 us; the launch traced here: 470 us
  waiting for transfers between devices  255 us (54%)
  other arithmetic  89.5 us (19%)
  blocking collectives  41 us (9%)
  starting transfers between devices  37 us (8%)
  local copies, waits for them, and re-layouts  16.9 us (4%)
  between operations  16.8 us (4%)
  matrix products  13.7 us (3%)
    psum x1, waiting for transfers between devices, on_device(): lax.psum(gram_of(ortho_basis, mapped), ('tier', 'row')) * inverse_rows  127 us
    psum x1, waiting for transfers between devices, on_device(): lax.psum(gram_of(stacked, stacked), ('tier', 'row')) * inverse_rows  123 us
    another operation x10, other arithmetic, on_device(): jnp.linalg.cholesky(lax.psum(gram_of(stacked, stacked), ('tier', 'row'))...  56.4 us
    psum x1, blocking collectives, on_device(): lax.psum((jnp.sum(current_modes * mode_image, 0), jnp.sum(current_modes *...  41 us
    another operation x4, other arithmetic, lower_solve(): return jax.scipy.linalg.solve_triangular(factor, matrix.T, lower=True).T  29.5 us
    ppermute x7, starting transfers between devices, shifted(): lax.ppermute(value, axis, [(source, source + steps) for source in range(f...  17.8 us
    ppermute x4, starting transfers between devices, with_halo(): before = lax.ppermute(last, axis, up)  13.9 us
  transfers between devices with their start and end apart: 17, of which 5 were waited for; matrix products, arithmetic and copies ran while one was open for 2% of the time, Pallas kernels for 0%

commit v1 on v0

v1 whole, which is shorter than its diff:
```python
import functools

import jax
import jax.numpy as jnp
from jax import lax
from jax.experimental import pallas as pl
from jax.experimental.pallas import tpu as pltpu
from jax.sharding import PartitionSpec as P

F32 = jnp.float32
BF16 = jnp.bfloat16
MESH = pl.DeviceIdType.MESH


def dot(a, b):
    return jnp.dot(a, b, preferred_element_type=F32)


def dot_t(a, b):
    return lax.dot_general(a, b, (((0,), (0,)), ((), ())), preferred_element_type=F32)


def halves(x):
    high = x.astype(BF16)
    return high, (x - high.astype(F32)).astype(BF16)


def dot3(a, b, product=dot):
    (a_high, a_low), (b_high, b_low) = halves(a), halves(b)
    return product(a_high, b_high) + (product(a_high, b_low) + product(a_low, b_high))


def flag(condition):
    return jnp.where(condition, 1.0, 0.0).astype(F32)


def scaled(tile, factor):
    return (tile.astype(F32) * factor).astype(BF16)


F_PREV, F_NEXT, F_LOW, F_UP, T_PREV, T_NEXT, T_LOW, P_UP, W_PREV, W_NEXT, W_LOW, W_UP, QUOT = range(13)
SUM_AT, SHARE_AT = 13, 16
SEMS = 19


def step_kernel(
    tiers, rows, cuts,
    cm, pv, diag, lat, lat_at, vert, vert_at, smo,
    w_out, early, mid, late,
    f_own, f_prev, f_next, f_low, f_up,
    t_prev, t_next, t_low, got_prev, got_next, got_up,
    p_own, p_low, wb, wb_prev, wb_next, wb_low, wb_up,
    q_buf, src0, src1, src2, box0, box1, box2,
    send_sem, recv_sem,
):
    tier, row = lax.axis_index("tier"), lax.axis_index("row")
    count = tiers * rows
    me = tier * rows + row
    bt = diag.shape[-1]
    k = cm.shape[1]

    def place(d):
        return (lax.div(d, rows), lax.rem(d, rows))

    def others(body):
        def step(i, carry):
            body(lax.rem(me + i, count))
            return carry
        lax.fori_loop(1, count, step, 0)

    barrier = pltpu.get_barrier_semaphore()
    others(lambda d: pl.semaphore_signal(barrier, inc=1, device_id=place(d), device_id_type=MESH))

    def remote(src, dst, slot, device):
        return pltpu.make_async_remote_copy(
            src_ref=src, dst_ref=dst, send_sem=send_sem.at[slot], recv_sem=recv_sem.at[slot],
            device_id=device, device_id_type=MESH)

    has_prev, has_next = row > 0, row < rows - 1
    has_low, has_up = tier > 0, tier < tiers - 1
    PREV, NEXT = (has_prev, has_next, (tier, row - 1)), (has_next, has_prev, (tier, row + 1))
    LOW, UP = (has_low, has_up, (tier - 1, row)), (has_up, has_low, (tier + 1, row))

    def send(src, dst, slot, way):
        @pl.when(way[0])
        def _():
            remote(src, dst, slot, way[2]).start()

    def receive(src, dst, slot, way):
        @pl.when(way[1])
        def _():
            remote(src, dst, slot, (tier, row)).wait_recv()

    def sent(src, dst, slot, way):
        @pl.when(way[0])
        def _():
            remote(src, dst, slot, (tier, row)).wait_send()

    f_own[:, :k] = cm[...].astype(BF16)
    f_own[:, k:] = pv[...].astype(BF16)
    below = flag(lat_at[1, 0] == 0)
    inner_low = 1.0 - below
    above = flag(lat_at[0, 1] == 3)
    inner_up = 1.0 - above
    t_prev[:bt] = lat[0, 0]
    t_prev[bt:] = scaled(lat[1, 0], below)
    t_next[:bt] = scaled(lat[0, 1], above)
    t_next[bt:] = lat[1, 1]
    for g in range(2):
        swap = flag(vert_at[g] == 1)
        t_low[g * bt:(g + 1) * bt, :bt] = scaled(vert[g], 1.0 - swap)
        t_low[g * bt:(g + 1) * bt, bt:] = scaled(vert[g], swap)

    @pl.when(jnp.logical_not(has_prev))
    def _():
        f_prev[...] = jnp.zeros_like(f_prev)
        wb_prev[...] = jnp.zeros_like(wb_prev)
        got_prev[...] = jnp.zeros_like(got_prev)

    @pl.when(jnp.logical_not(has_next))
    def _():
        f_next[...] = jnp.zeros_like(f_next)
        wb_next[...] = jnp.zeros_like(wb_next)
        got_next[...] = jnp.zeros_like(got_next)

    @pl.when(jnp.logical_not(has_low))
    def _():
        f_low[...] = jnp.zeros_like(f_low)
        wb_low[...] = jnp.zeros_like(wb_low)
        p_low[...] = jnp.zeros_like(p_low)

    @pl.when(jnp.logical_not(has_up))
    def _():
        f_up[...] = jnp.zeros_like(f_up)
        wb_up[...] = jnp.zeros_like(wb_up)
        got_up[...] = jnp.zeros_like(got_up)

    first = [
        (f_own, f_up, F_LOW, LOW), (f_own, f_low, F_UP, UP),
        (f_own, f_next, F_PREV, PREV), (f_own, f_prev, F_NEXT, NEXT),
        (t_low, got_up, T_LOW, LOW), (t_prev, got_next, T_PREV, PREV), (t_next, got_prev, T_NEXT, NEXT),
    ]
    second = [
        (wb, wb_up, W_LOW, LOW), (wb, wb_low, W_UP, UP),
        (wb, wb_next, W_PREV, PREV), (wb, wb_prev, W_NEXT, NEXT),
    ]
    pl.semaphore_wait(barrier, count - 1)
    for item in first:
        send(*item)

    zero = jnp.zeros((bt, bt), BF16)
    cross_up, cross_low = scaled(lat[0, 1], inner_up), scaled(lat[1, 0], inner_low)
    inner = jnp.concatenate([
        jnp.concatenate([diag[0], cross_up], 1), jnp.concatenate([cross_low, diag[1]], 1)], 0)
    crossed = jnp.concatenate([
        jnp.concatenate([zero, cross_up], 1), jnp.concatenate([cross_low, zero], 1)], 0)

    def local(own):
        return dot(inner, own) + dot_t(crossed, own)

    def coupled(total, prev, after, low, up):
        total = total + dot(t_prev[...], prev[bt:]) + dot(t_next[...], after[:bt])
        total = total + dot(t_low[...], low[...]) + dot_t(got_up[...], up[...])
        edge = jnp.concatenate([dot_t(got_prev[...], prev[...]), dot_t(got_next[...], after[...])], 0)
        return total + edge

    def spread(src, box, which):
        chunk, owners = cuts[which]
        def body(d):
            @pl.when(d < owners)
            def _():
                remote(src.at[pl.ds(pl.multiple_of(d * chunk, 8), chunk)], box.at[me], SUM_AT + which, place(d)).start()
        others(body)
        @pl.when(me < owners)
        def _():
            box[pl.ds(me, 1)] = src[pl.ds(pl.multiple_of(me * chunk, 8), chunk)][None]

    def share(src, box, out, which):
        chunk, owners = cuts[which]
        @pl.when(me < owners)
        def _():
            everything = box.at[pl.ds(0, count - 1)]
            remote(everything, everything, SUM_AT + which, (tier, row)).wait_recv()
            mine = pl.ds(pl.multiple_of(me * chunk, 8), chunk)
            out[mine] = jnp.sum(box[...], axis=0)
            others(lambda d: remote(out.at[mine], out.at[mine], SHARE_AT + which, place(d)).start())

    def gathered(src, box, out, which):
        chunk, owners = cuts[which]
        def arrive(number):
            part = out.at[pl.ds(0, number * chunk)]
            remote(part, part, SHARE_AT + which, (tier, row)).wait_recv()
            part = src.at[pl.ds(0, number * chunk)]
            remote(part, part, SUM_AT + which, (tier, row)).wait_send()
        @pl.when(me < owners)
        def _():
            arrive(owners - 1)
            everything = box.at[pl.ds(0, count - 1)]
            remote(everything, everything, SHARE_AT + which, (tier, row)).wait_send()
        @pl.when(me >= owners)
        def _():
            arrive(owners)

    total = local(f_own[...])
    for item in first:
        receive(*item)
    image = coupled(total, f_prev, f_next, f_low, f_up)
    x, mode_image = cm[...], image[:, :k]
    q_buf[pl.ds(me, 1), 0:1] = jnp.sum(x * mode_image, 0, keepdims=True)[None]
    q_buf[pl.ds(me, 1), 1:2] = jnp.sum(x * x, 0, keepdims=True)[None]
    others(lambda d: remote(q_buf.at[me], q_buf.at[me], QUOT, place(d)).start())

    pair = jnp.concatenate([mode_image, x], 1)
    receive(p_own, p_low, P_UP, UP)
    low_high, low_low = halves(p_low[...])
    pair = pair - (dot(t_low[...], low_high) + dot(t_low[...], low_low))
    p_own[:bt] = dot3(smo[0], pair[:bt])
    p_own[bt:] = dot3(smo[1], pair[bt:])
    send(p_own, p_low, P_UP, UP)

    fields = jnp.concatenate([x, pv[...]], 1)
    given = jnp.concatenate([fields, image], 1)
    product = dot3(fields, given, dot_t)
    src0[0 * k:1 * k] = product[:k, :k]
    src0[1 * k:2 * k] = product[:k, k:2 * k]
    src0[2 * k:3 * k] = product[k:, k:2 * k]
    src0[3 * k:4 * k] = product[:k, 2 * k:3 * k]
    src0[4 * k:5 * k] = product[k:, 2 * k:3 * k]
    src0[5 * k:6 * k] = product[k:, 3 * k:]
    src1[0 * k:1 * k] = product[:k, 3 * k:]
    spread(src0, box0, 0)

    everyone = q_buf.at[pl.ds(0, count - 1)]
    remote(everyone, everyone, QUOT, (tier, row)).wait_recv()
    sums = jnp.sum(q_buf[...], axis=0)
    w = p_own[:, :k] - p_own[:, k:] * (sums[0:1] / sums[1:2])
    w_out[...] = w
    wb[...] = w.astype(BF16)
    for item in second:
        send(*item)

    product = dot3(w, jnp.concatenate([given, w], 1), dot_t)
    for at in range(5):
        src1[(at + 1) * k:(at + 2) * k] = product[:, at * k:(at + 1) * k]
    spread(src1, box1, 1)
    total = local(wb[...])
    for item in second:
        receive(*item)
    work_image = coupled(total, wb_prev, wb_next, wb_low, wb_up)
    product = dot3(jnp.concatenate([fields, w], 1), work_image, dot_t)
    src2[...] = product
    spread(src2, box2, 2)
    share(src0, box0, early, 0)
    share(src1, box1, mid, 1)
    share(src2, box2, late, 2)
    gathered(src0, box0, early, 0)
    gathered(src1, box1, mid, 1)
    gathered(src2, box2, late, 2)
    remote(everyone, everyone, QUOT, (tier, row)).wait_send()
    for item in first + second:
        sent(*item)
    sent(p_own, p_low, P_UP, UP)


def basis_kernel(
    inverse_rows, early, mid, late, cm, w, pv, ortho, projected, z_ref, a_ref, m_ref
):
    k = cm.shape[1]
    n = 3 * k

    def at(ref, i):
        return ref[i * k:(i + 1) * k]

    xw, xp, wp = at(mid, 1).T, at(early, 1), at(mid, 2)
    gram = jnp.concatenate([
        jnp.concatenate([at(early, 0), xw, xp], 1),
        jnp.concatenate([at(mid, 1), at(mid, 5), wp], 1),
        jnp.concatenate([xp.T, wp.T, at(early, 2)], 1)], 0) * inverse_rows
    inner = jnp.concatenate([
        jnp.concatenate([at(early, 3), at(late, 0), at(mid, 0)], 1),
        jnp.concatenate([at(mid, 3), at(late, 2), at(mid, 4)], 1),
        jnp.concatenate([at(early, 4), at(late, 1), at(early, 5)], 1)], 0) * inverse_rows
    below = lax.broadcasted_iota(jnp.int32, (n, n), 0)
    across = lax.broadcasted_iota(jnp.int32, (n, n), 1)
    on_diagonal = below == across
    eye = on_diagonal.astype(F32)
    weights = jnp.where(below < across, 1.0, jnp.where(on_diagonal, 0.5, 0.0))
    marked = gram * eye
    scale_row = lax.rsqrt(jnp.sum(marked, 0, keepdims=True))
    scale_column = lax.rsqrt(jnp.sum(marked, 1, keepdims=True))
    a_ref[...] = gram * scale_row * scale_column

    def error(z, split):
        a = a_ref[...]
        if split:
            return dot3(z, dot3(a, z), dot_t) - eye
        z = z.astype(BF16)
        return dot_t(z, dot(a.astype(BF16), z).astype(BF16)) - eye

    z_ref[...] = eye - (a_ref[...] - eye) * weights
    for _ in range(2):
        z = z_ref[...]
        move = error(z, False) * weights
        z_ref[...] = z - dot(z.astype(BF16), move.astype(BF16))

    def going(state):
        return jnp.logical_and(state[0] < 8, jnp.logical_not(state[1] < 2e-4))

    def step(state):
        z = z_ref[...]
        now = error(z, True)
        z_ref[...] = z - dot3(z, now * weights)
        return state[0] + 1, jnp.max(jnp.abs(now))

    _, left = lax.while_loop(going, step, (jnp.int32(0), jnp.float32(1.0)))
    lowest = jnp.min(jnp.where(on_diagonal, z_ref[...], 1.0))
    good = jnp.logical_and(left < 2e-4, lowest > 0.0)

    @pl.when(jnp.logical_not(good))
    def _():
        m_ref[...] = eye
        rows_at = lax.broadcasted_iota(jnp.int32, (n, 1), 0)

        def column(j, carry):
            row_a, row_m = a_ref[pl.ds(j, 1), :], m_ref[pl.ds(j, 1), :]
            a = a_ref[...]
            cut = jnp.sum(jnp.where(across == j, a, 0.0), 1, keepdims=True)
            pivot = jnp.sum(jnp.where(rows_at == j, cut, 0.0), 0, keepdims=True)
            factor = lax.rsqrt(pivot)
            row_a, row_m, cut = row_a * factor, row_m * factor, jnp.where(rows_at > j, cut * factor, 0.0)
            a_ref[...] = a - cut * row_a
            m_ref[...] = m_ref[...] - cut * row_m
            m_ref[pl.ds(j, 1), :] = row_m
            return carry

        lax.fori_loop(0, n, column, 0)
        z_ref[...] = m_ref[...].T

    inverse = z_ref[...] * scale_column
    high, low = halves(inverse)
    stacked = jnp.concatenate([cm[...], w[...], pv[...]], 1)
    s_high, s_low = halves(stacked)
    ortho[...] = dot(s_high, high) + (dot(s_high, low) + dot(s_low, high))
    half = dot3(inner, inverse)
    projected[...] = dot3(inverse, half, dot_t)


def vmem(count):
    return [pl.BlockSpec(memory_space=pltpu.VMEM)] * count


def on_device(
    current_modes, previous, diag_tiles, lateral_tiles, lateral_index, vertical_tiles, vertical_index, smoother
):
    tiers, rows = lax.axis_size("tier"), lax.axis_size("row")
    count = tiers * rows
    height, k = current_modes.shape
    bt = diag_tiles.shape[-1]
    cuts = []
    for total in (6 * k, 6 * k, 3 * k):
        chunk = 8
        while chunk * count < total or total % chunk:
            chunk += 8
        cuts.append((chunk, total // chunk))
    smem = pl.BlockSpec(memory_space=pltpu.SMEM)
    one = pl.BlockSpec(memory_space=pltpu.VMEM)
    pair = pltpu.VMEM((height, 2 * k), BF16)
    single = pltpu.VMEM((height, k), BF16)
    tall = pltpu.VMEM((height, bt), BF16)
    square = pltpu.VMEM((height, height), BF16)
    wide = pltpu.VMEM((height, 2 * k), F32)
    w, early, mid, late = pl.pallas_call(
        functools.partial(step_kernel, tiers, rows, cuts),
        out_shape=[
            jax.ShapeDtypeStruct((height, k), F32), jax.ShapeDtypeStruct((6 * k, k), F32),
            jax.ShapeDtypeStruct((6 * k, k), F32), jax.ShapeDtypeStruct((3 * k, k), F32)],
        in_specs=[one, one, one, one, smem, one, smem, one],
        out_specs=vmem(4),
        scratch_shapes=[
            pair, pair, pair, pair, pair,
            tall, tall, square, tall, tall, square,
            wide, wide, single, single, single, single, single,
            pltpu.VMEM((count, 8, k), F32),
            pltpu.VMEM((6 * k, k), F32), pltpu.VMEM((6 * k, k), F32), pltpu.VMEM((3 * k, k), F32),
        ] + [pltpu.VMEM((count, chunk, k), F32) for chunk, _ in cuts] + [
            pltpu.SemaphoreType.DMA((SEMS,)), pltpu.SemaphoreType.DMA((SEMS,))],
        compiler_params=pltpu.CompilerParams(
            collective_id=0, has_side_effects=True, vmem_limit_bytes=40 * 2**20),
        name="step",
    )(
        current_modes, previous, diag_tiles[0, 0], lateral_tiles[0, 0], lateral_index[0, 0],
        vertical_tiles[0, 0], vertical_index[0, 0], smoother[0, 0])
    n = 3 * k
    full = pltpu.VMEM((n, n), F32)
    return pl.pallas_call(
        functools.partial(basis_kernel, 1.0 / (height * count)),
        out_shape=[jax.ShapeDtypeStruct((height, n), F32), jax.ShapeDtypeStruct((n, n), F32)],
        in_specs=vmem(6),
        out_specs=vmem(2),
        scratch_shapes=[full, full, full],
        compiler_params=pltpu.CompilerParams(vmem_limit_bytes=40 * 2**20),
        name="basis",
    )(early, mid, late, current_modes, w, previous)


def solution(mesh):
    placed = (
        P(("tier", "row"), None),
        P(("tier", "row"), None),
        P("tier", "row", None, None, None),
        P("tier", "row", None, None, None, None),
        P("tier", "row", None, None),
        P("tier", "row", None, None, None),
        P("tier", "row", None),
        P("tier", "row", None, None, None),
    )
    return jax.shard_map(
        on_device,
        mesh=mesh,
        in_specs=placed,
        out_specs=(P(("tier", "row"), None), P()),
        check_vma=False,
    )
```

time: 471 us -> 237 us (0.50)
  waiting for transfers between devices: 255 us -> 0 us
  Pallas kernels: 0 us -> 227 us
  other arithmetic: 89.5 us -> 0 us
  blocking collectives: 41 us -> 0 us
  starting transfers between devices: 37 us -> 0 us
  between operations: 16.8 us -> 0.66 us
  matrix products: 13.7 us -> 0 us
  local copies, waits for them, and re-layouts: 16.9 us -> 5.96 us
    psum x2 -> x0, waiting for transfers between devices: 249 us -> none  [the longest x1 127 us: on_device(): lax.psum(gram_of(ortho_basis, mapped), ('tier', 'row')) * inverse_rows]
    pallas_call x0 -> x2, Pallas kernels: none -> 227 us  [the longest x1 157 us: on_device(): pl.pallas_call(functools.partial(basis_kernel, 1.0 / (height * count)), o...]
    another operation x16 -> x0, other arithmetic: 86.9 us -> none  [the longest x10 56.4 us: on_device(): jnp.linalg.cholesky(lax.psum(gram_of(stacked, stacked), ('tier', 'row'))...]
    psum x1 -> x0, blocking collectives: 41 us -> none  [on_device(): lax.psum((jnp.sum(current_modes * mode_image, 0), jnp.sum(current_modes *...]
    ppermute x15 -> x0, starting transfers between devices: 36.9 us -> none  [the longest x7 17.8 us: shifted(): lax.ppermute(value, axis, [(source, source + steps) for source in range(f...]
    dot_general x20 -> x0, matrix products: 8.84 us -> none  [the longest x2 3.27 us: gram_of(): return jnp.dot(left_side.T, right_side, precision=lax.Precision.HIGHEST)]
    another operation x13 -> x0, local copies, waits for them, and re-layouts: 6.02 us -> none  [the longest x10 5.96 us: lower_solve(): return jax.scipy.linalg.solve_triangular(factor, matrix.T, lower=True).T]
    ppermute x15 -> x0, waiting for transfers between devices: 5.6 us -> none  [the longest x7 5.58 us: shifted(): lax.ppermute(value, axis, [(source, source + steps) for source in range(f...]
  transfers between devices with their start and end apart: 17 -> 0, of which waited for: 5 -> 0; matrix products, arithmetic and copies ran while one was open for 2% -> 0% of each run, Pallas kernels for 0% -> 0%
where the time goes in v1:
time: 237 us; the launch traced here: 233 us
  Pallas kernels  227 us (96%)
  local copies, waits for them, and re-layouts  5.96 us (3%)
    pallas_call x1, Pallas kernels, on_device(): pl.pallas_call(functools.partial(basis_kernel, 1.0 / (height * count)), o...  157 us
    pallas_call x1, Pallas kernels, on_device(): pl.pallas_call(functools.partial(step_kernel, tiers, rows, cuts), out_sha...  69.6 us
    unnamed x16, local copies, waits for them, and re-layouts  5.96 us

profile of v1, /device:TPU:0, one launch (start us, length us, event | category | flops | bytes accessed | tf_op | source)
XLA Modules:
  0.0 233.4 jit_solution(16027313712478819256)
XLA Ops:
  0.6 0.0 copy-start.6
  0.6 0.0 copy-start.7
  0.7 0.7 copy-done.6
  1.3 0.0 copy-done.7
  1.3 0.0 copy-start
  1.3 0.9 copy-done
  2.2 0.0 copy-start.1
  2.2 0.9 copy-done.1
  3.1 0.0 copy-start.2
  3.1 0.9 copy-done.2
  4.0 0.0 copy-start.3
  4.0 0.9 copy-done.3
  4.9 0.0 copy-start.4
  4.9 0.8 copy-done.4
  5.8 0.0 copy-start.5
  5.8 0.8 copy-done.5
  6.6 69.6 %step.1 = (f32[256,128]{1,0:T(8,128)S(1)}, f32[768,128]{1,0:T(8,128)S(1)}, f32[768,128]{1,0:T(8,128)S(1)}, f32[384,128]{1,0:T(8,128)S(1)}) custom-call(f32[256,128]{1,0:T(8,128)S(1)} %copy-done, f32[256,128]{1,0:T(8,128)S(1)} %copy-done.1, bf16[2,128,128]{2,1,0:T(8,128)(2,1)S(1)} %bitcast.8, bf16[2,2,128,128]{3,2,1,0:T(8,128)(2,1)S(1)} %bitcast.6, ...), custom_call_target="tpu_custom_call" | custom-call | tf_op jit(solution)/shard_map/step/pallas_call | solution.py:372
  76.2 157.2 %basis.1 = (f32[256,384]{1,0:T(8,128)}, f32[384,384]{1,0:T(8,128)}) custom-call(f32[768,128]{1,0:T(8,128)S(1)} %get-tuple-element.6.early, f32[768,128]{1,0:T(8,128)S(1)} %get-tuple-element.7.mid, f32[384,128]{1,0:T(8,128)S(1)} %get-tuple-element.8.late, f32[256,128]{1,0:T(8,128)S(1)} %copy-done, f32[256,128]{1,0:T(8,128)S(1)} %get-tuple-element.9.w, ...), custom_call_target="tpu_custom_call" | custom-call | tf_op jit(solution)/shard_map/basis/pallas_call | solution.py:395
Async XLA Ops:
  0.6 0.7 copy-start.6
  0.6 0.7 copy-start.7
  1.3 0.9 copy-start
  2.2 0.9 copy-start.1
  3.1 0.9 copy-start.2
  4.0 0.9 copy-start.3
  4.9 0.8 copy-start.4
  5.8 0.8 copy-start.5

commit v2 on v1

--- a/solution.py
+++ b/solution.py
@@ -38,20 +38,19 @@
     return (tile.astype(F32) * factor).astype(BF16)
 
 
-F_PREV, F_NEXT, F_LOW, F_UP, T_PREV, T_NEXT, T_LOW, P_UP, W_PREV, W_NEXT, W_LOW, W_UP, QUOT = range(13)
-SUM_AT, SHARE_AT = 13, 16
-SEMS = 19
+F_PREV, F_NEXT, F_LOW, F_UP, T_PREV, T_NEXT, T_LOW, P_UP, W_PREV, W_NEXT, W_LOW, W_UP, QUOT, X_UP = range(14)
+SUM_AT = 14
+SEMS = SUM_AT + 18
 
 
 def step_kernel(
-    tiers, rows, cuts,
+    tiers, rows,
     cm, pv, diag, lat, lat_at, vert, vert_at, smo,
     w_out, early, mid, late,
     f_own, f_prev, f_next, f_low, f_up,
     t_prev, t_next, t_low, got_prev, got_next, got_up,
-    p_own, p_low, wb, wb_prev, wb_next, wb_low, wb_up,
-    q_buf, src0, src1, src2, box0, box1, box2,
-    send_sem, recv_sem,
+    p_own, p_low, x_own, x_low, wb, wb_prev, wb_next, wb_low, wb_up,
+    q_buf, src0, src1, src2, send_sem, recv_sem, *boxes,
 ):
     tier, row = lax.axis_index("tier"), lax.axis_index("row")
     count = tiers * rows
@@ -128,6 +127,7 @@
         f_low[...] = jnp.zeros_like(f_low)
         wb_low[...] = jnp.zeros_like(wb_low)
         p_low[...] = jnp.zeros_like(p_low)
+        x_low[...] = jnp.zeros_like(x_low)
 
     @pl.when(jnp.logical_not(has_up))
     def _():
@@ -164,42 +164,108 @@
         edge = jnp.concatenate([dot_t(got_prev[...], prev[...]), dot_t(got_next[...], after[...])], 0)
         return total + edge
 
-    def spread(src, box, which):
-        chunk, owners = cuts[which]
-        def body(d):
-            @pl.when(d < owners)
-            def _():
-                remote(src.at[pl.ds(pl.multiple_of(d * chunk, 8), chunk)], box.at[me], SUM_AT + which, place(d)).start()
-        others(body)
-        @pl.when(me < owners)
-        def _():
-            box[pl.ds(me, 1)] = src[pl.ds(pl.multiple_of(me * chunk, 8), chunk)][None]
-
-    def share(src, box, out, which):
-        chunk, owners = cuts[which]
-        @pl.when(me < owners)
-        def _():
-            everything = box.at[pl.ds(0, count - 1)]
-            remote(everything, everything, SUM_AT + which, (tier, row)).wait_recv()
-            mine = pl.ds(pl.multiple_of(me * chunk, 8), chunk)
-            out[mine] = jnp.sum(box[...], axis=0)
-            others(lambda d: remote(out.at[mine], out.at[mine], SHARE_AT + which, place(d)).start())
-
-    def gathered(src, box, out, which):
-        chunk, owners = cuts[which]
-        def arrive(number):
-            part = out.at[pl.ds(0, number * chunk)]
-            remote(part, part, SHARE_AT + which, (tier, row)).wait_recv()
-            part = src.at[pl.ds(0, number * chunk)]
-            remote(part, part, SUM_AT + which, (tier, row)).wait_send()
-        @pl.when(me < owners)
-        def _():
-            arrive(owners - 1)
-            everything = box.at[pl.ds(0, count - 1)]
-            remote(everything, everything, SHARE_AT + which, (tier, row)).wait_send()
-        @pl.when(me >= owners)
-        def _():
-            arrive(owners)
+    half_at = lax.rem(row, 2)
+    plane_at = tier * 2 + lax.rem(lax.div(row, 2), 2)
+    line_at = lax.div(row, 4)
+    planes, lines = 2 * tiers, rows // 4
+    buddy = (tier, row + 1 - 2 * half_at)
+
+    def plane_place(j):
+        return (lax.div(j, 2), line_at * 4 + lax.rem(j, 2) * 2 + half_at)
+
+    def line_place(j):
+        return (tier, j * 4 + lax.rem(row, 4))
+
+    def around(size, own, body):
+        def step(i, carry):
+            body(lax.rem(own + i, size))
+            return carry
+        lax.fori_loop(1, size, step, 0)
+
+    def arrived(part, slot):
+        remote(part, part, slot, (tier, row)).wait_recv()
+
+    def left(part, slot):
+        remote(part, part, slot, (tier, row)).wait_send()
+
+    class Sum:
+        def __init__(self, which, src, part1, part2, box1, box2, box3, out):
+            self.src, self.part1, self.part2, self.out = src, part1, part2, out
+            self.box1, self.box2, self.box3 = box1, box2, box3
+            self.slot = SUM_AT + 6 * which
+            self.n1 = src.shape[0] // 2
+            self.n2 = self.n1 // planes
+            self.n3 = self.n2 // lines
+            self.at1 = pl.multiple_of(half_at * self.n1, 8)
+            self.at2 = pl.multiple_of(self.at1 + plane_at * self.n2, 8)
+            self.at3 = pl.multiple_of(self.at2 + line_at * self.n3, 8)
+
+        def send1(self):
+            away = pl.multiple_of((1 - half_at) * self.n1, 8)
+            remote(self.src.at[pl.ds(away, self.n1)], self.box1, self.slot, buddy).start()
+
+        def send2(self):
+            arrived(self.box1, self.slot)
+            self.part1[...] = self.src[pl.ds(self.at1, self.n1)] + self.box1[...]
+            def body(j):
+                piece = self.part1.at[pl.ds(pl.multiple_of(j * self.n2, 8), self.n2)]
+                remote(piece, self.box2.at[plane_at], self.slot + 1, plane_place(j)).start()
+            around(planes, plane_at, body)
+            mine = self.part1[pl.ds(pl.multiple_of(plane_at * self.n2, 8), self.n2)]
+            self.box2[pl.ds(plane_at, 1)] = mine[None]
+
+        def send3(self):
+            arrived(self.box2.at[pl.ds(0, planes - 1)], self.slot + 1)
+            self.part2[...] = jnp.sum(self.box2[...], axis=0)
+            def body(j):
+                piece = self.part2.at[pl.ds(pl.multiple_of(j * self.n3, 8), self.n3)]
+                remote(piece, self.box3.at[line_at], self.slot + 2, line_place(j)).start()
+            around(lines, line_at, body)
+            mine = self.part2[pl.ds(pl.multiple_of(line_at * self.n3, 8), self.n3)]
+            self.box3[pl.ds(line_at, 1)] = mine[None]
+
+        def share3(self):
+            arrived(self.box3.at[pl.ds(0, lines - 1)], self.slot + 2)
+            part = self.out.at[pl.ds(self.at3, self.n3)]
+            self.out[pl.ds(self.at3, self.n3)] = jnp.sum(self.box3[...], axis=0)
+            around(lines, line_at, lambda j: remote(part, part, self.slot + 3, line_place(j)).start())
+
+        def share2(self):
+            arrived(self.out.at[pl.ds(0, self.n2 - self.n3)], self.slot + 3)
+            part = self.out.at[pl.ds(self.at2, self.n2)]
+            around(planes, plane_at, lambda j: remote(part, part, self.slot + 4, plane_place(j)).start())
+
+        def share1(self):
+            arrived(self.out.at[pl.ds(0, self.n1 - self.n2)], self.slot + 4)
+            part = self.out.at[pl.ds(self.at1, self.n1)]
+            remote(part, part, self.slot + 5, buddy).start()
+
+        def end(self):
+            whole = self.out.at[pl.ds(0, self.n1)]
+            arrived(whole, self.slot + 5)
+            left(whole, self.slot + 5)
+            left(self.out.at[pl.ds(0, self.n1 - self.n2)], self.slot + 4)
+            left(self.out.at[pl.ds(0, self.n2 - self.n3)], self.slot + 3)
+            left(self.box3.at[pl.ds(0, lines - 1)], self.slot + 2)
+            left(self.box2.at[pl.ds(0, planes - 1)], self.slot + 1)
+            left(self.box1, self.slot)
+
+    first_sum = Sum(0, src0, *boxes[0:5], early)
+    second_sum = Sum(1, src1, *boxes[5:10], mid)
+    third_sum = Sum(2, src2, *boxes[10:15], late)
+
+    def smooth(field, low_ref, out):
+        low_high, low_low = halves(low_ref[...])
+        field = field - (dot(t_low[...], low_high) + dot(t_low[...], low_low))
+        out[:bt] = dot3(smo[0], field[:bt])
+        out[bt:] = dot3(smo[1], field[bt:])
+
+    @pl.when(jnp.logical_not(has_low))
+    def _():
+        smooth(cm[...], x_low, x_own)
+    @pl.when(jnp.logical_and(jnp.logical_not(has_low), has_up))
+    def _():
+        remote(x_own, x_low, X_UP, UP[2]).start()
 
     total = local(f_own[...])
     for item in first:
@@ -210,12 +276,15 @@
     q_buf[pl.ds(me, 1), 1:2] = jnp.sum(x * x, 0, keepdims=True)[None]
     others(lambda d: remote(q_buf.at[me], q_buf.at[me], QUOT, place(d)).start())
 
-    pair = jnp.concatenate([mode_image, x], 1)
+    @pl.when(has_low)
+    def _():
+        arrived(x_low, X_UP)
+        smooth(cm[...], x_low, x_own)
+    @pl.when(jnp.logical_and(has_low, has_up))
+    def _():
+        remote(x_own, x_low, X_UP, UP[2]).start()
     receive(p_own, p_low, P_UP, UP)
-    low_high, low_low = halves(p_low[...])
-    pair = pair - (dot(t_low[...], low_high) + dot(t_low[...], low_low))
-    p_own[:bt] = dot3(smo[0], pair[:bt])
-    p_own[bt:] = dot3(smo[1], pair[bt:])
+    smooth(mode_image, p_low, p_own)
     send(p_own, p_low, P_UP, UP)
 
     fields = jnp.concatenate([x, pv[...]], 1)
@@ -228,12 +297,12 @@
     src0[4 * k:5 * k] = product[k:, 2 * k:3 * k]
     src0[5 * k:6 * k] = product[k:, 3 * k:]
     src1[0 * k:1 * k] = product[:k, 3 * k:]
-    spread(src0, box0, 0)
+    first_sum.send1()
 
     everyone = q_buf.at[pl.ds(0, count - 1)]
     remote(everyone, everyone, QUOT, (tier, row)).wait_recv()
     sums = jnp.sum(q_buf[...], axis=0)
-    w = p_own[:, :k] - p_own[:, k:] * (sums[0:1] / sums[1:2])
+    w = p_own[...] - x_own[...] * (sums[0:1] / sums[1:2])
     w_out[...] = w
     wb[...] = w.astype(BF16)
     for item in second:
@@ -242,24 +311,37 @@
     product = dot3(w, jnp.concatenate([given, w], 1), dot_t)
     for at in range(5):
         src1[(at + 1) * k:(at + 2) * k] = product[:, at * k:(at + 1) * k]
-    spread(src1, box1, 1)
+    second_sum.send1()
+    first_sum.send2()
     total = local(wb[...])
     for item in second:
         receive(*item)
     work_image = coupled(total, wb_prev, wb_next, wb_low, wb_up)
     product = dot3(jnp.concatenate([fields, w], 1), work_image, dot_t)
-    src2[...] = product
-    spread(src2, box2, 2)
-    share(src0, box0, early, 0)
-    share(src1, box1, mid, 1)
-    share(src2, box2, late, 2)
-    gathered(src0, box0, early, 0)
-    gathered(src1, box1, mid, 1)
-    gathered(src2, box2, late, 2)
+    src2[:3 * k] = product
+    third_sum.send1()
+    second_sum.send2()
+    first_sum.send3()
+    third_sum.send2()
+    second_sum.send3()
+    first_sum.share3()
+    third_sum.send3()
+    second_sum.share3()
+    first_sum.share2()
+    third_sum.share3()
+    second_sum.share2()
+    first_sum.share1()
+    third_sum.share2()
+    second_sum.share1()
+    third_sum.share1()
+    first_sum.end()
+    second_sum.end()
+    third_sum.end()
     remote(everyone, everyone, QUOT, (tier, row)).wait_send()
     for item in first + second:
         sent(*item)
     sent(p_own, p_low, P_UP, UP)
+    sent(x_own, x_low, X_UP, UP)
 
 
 def basis_kernel(
@@ -356,34 +438,36 @@
     count = tiers * rows
     height, k = current_modes.shape
     bt = diag_tiles.shape[-1]
-    cuts = []
-    for total in (6 * k, 6 * k, 3 * k):
-        chunk = 8
-        while chunk * count < total or total % chunk:
-            chunk += 8
-        cuts.append((chunk, total // chunk))
+    unit = 8 * count
+    totals = [-(-blocks * k // unit) * unit for blocks in (6, 6, 3)]
+    boxes = []
+    for total in totals:
+        n1 = total // 2
+        n2 = n1 // (2 * tiers)
+        n3 = n2 // (rows // 4)
+        for shape in ((n1, k), (n2, k), (n1, k), (2 * tiers, n2, k), (rows // 4, n3, k)):
+            boxes.append(pltpu.VMEM(shape, F32))
     smem = pl.BlockSpec(memory_space=pltpu.SMEM)
     one = pl.BlockSpec(memory_space=pltpu.VMEM)
     pair = pltpu.VMEM((height, 2 * k), BF16)
     single = pltpu.VMEM((height, k), BF16)
     tall = pltpu.VMEM((height, bt), BF16)
     square = pltpu.VMEM((height, height), BF16)
-    wide = pltpu.VMEM((height, 2 * k), F32)
+    wide = pltpu.VMEM((height, k), F32)
     w, early, mid, late = pl.pallas_call(
-        functools.partial(step_kernel, tiers, rows, cuts),
+        functools.partial(step_kernel, tiers, rows),
         out_shape=[
-            jax.ShapeDtypeStruct((height, k), F32), jax.ShapeDtypeStruct((6 * k, k), F32),
-            jax.ShapeDtypeStruct((6 * k, k), F32), jax.ShapeDtypeStruct((3 * k, k), F32)],
+            jax.ShapeDtypeStruct((height, k), F32)] + [
+            jax.ShapeDtypeStruct((total, k), F32) for total in totals],
         in_specs=[one, one, one, one, smem, one, smem, one],
         out_specs=vmem(4),
         scratch_shapes=[
             pair, pair, pair, pair, pair,
             tall, tall, square, tall, tall, square,
-            wide, wide, single, single, single, single, single,
+            wide, wide, wide, wide, single, single, single, single, single,
             pltpu.VMEM((count, 8, k), F32),
-            pltpu.VMEM((6 * k, k), F32), pltpu.VMEM((6 * k, k), F32), pltpu.VMEM((3 * k, k), F32),
-        ] + [pltpu.VMEM((count, chunk, k), F32) for chunk, _ in cuts] + [
-            pltpu.SemaphoreType.DMA((SEMS,)), pltpu.SemaphoreType.DMA((SEMS,))],
+        ] + [pltpu.VMEM((total, k), F32) for total in totals] + [
+            pltpu.SemaphoreType.DMA((SEMS,)), pltpu.SemaphoreType.DMA((SEMS,))] + boxes,
         compiler_params=pltpu.CompilerParams(
             collective_id=0, has_side_effects=True, vmem_limit_bytes=40 * 2**20),
         name="step",

time: 237 us -> 209 us (0.88); the launches traced: 233 us -> 209 us
  Pallas kernels: 227 us -> 202 us
    pallas_call x1, Pallas kernels: 69.6 us -> 45.2 us  [on_device(): pl.pallas_call(functools.partial(step_kernel, tiers, rows), out_shape=[ja...]
where the time goes in v2:
time: 209 us
  Pallas kernels  202 us (97%)
  local copies, waits for them, and re-layouts  5.96 us (3%)
    pallas_call x1, Pallas kernels, on_device(): pl.pallas_call(functools.partial(basis_kernel, 1.0 / (height * count)), o...  157 us
    pallas_call x1, Pallas kernels, on_device(): pl.pallas_call(functools.partial(step_kernel, tiers, rows), out_shape=[ja...  45.2 us
    unnamed x16, local copies, waits for them, and re-layouts  5.96 us

profile of v2, /device:TPU:0, one launch (start us, length us, event | category | flops | bytes accessed | tf_op | source)
XLA Modules:
  0.0 209.1 jit_solution(11194594486025909299)
XLA Ops:
  0.6 0.0 copy-start.6
  0.6 0.0 copy-start.7
  0.7 0.7 copy-done.6
  1.3 0.0 copy-done.7
  1.3 0.0 copy-start
  1.3 0.9 copy-done
  2.2 0.0 copy-start.1
  2.2 0.9 copy-done.1
  3.1 0.0 copy-start.2
  3.1 0.9 copy-done.2
  4.0 0.0 copy-start.3
  4.0 0.9 copy-done.3
  4.9 0.0 copy-start.4
  4.9 0.8 copy-done.4
  5.8 0.0 copy-start.5
  5.8 0.8 copy-done.5
  6.6 45.2 %step.1 = (f32[256,128]{1,0:T(8,128)S(1)}, f32[768,128]{1,0:T(8,128)S(1)}, f32[768,128]{1,0:T(8,128)S(1)}, f32[512,128]{1,0:T(8,128)S(1)}) custom-call(f32[256,128]{1,0:T(8,128)S(1)} %copy-done, f32[256,128]{1,0:T(8,128)S(1)} %copy-done.1, bf16[2,128,128]{2,1,0:T(8,128)(2,1)S(1)} %bitcast.8, bf16[2,2,128,128]{3,2,1,0:T(8,128)(2,1)S(1)} %bitcast.6, ...), custom_call_target="tpu_custom_call" | custom-call | tf_op jit(solution)/shard_map/step/pallas_call | solution.py:457
  51.9 157.2 %basis.1 = (f32[256,384]{1,0:T(8,128)}, f32[384,384]{1,0:T(8,128)}) custom-call(f32[768,128]{1,0:T(8,128)S(1)} %get-tuple-element.6.early, f32[768,128]{1,0:T(8,128)S(1)} %get-tuple-element.7.mid, f32[512,128]{1,0:T(8,128)S(1)} %get-tuple-element.8.late, f32[256,128]{1,0:T(8,128)S(1)} %copy-done, f32[256,128]{1,0:T(8,128)S(1)} %get-tuple-element.9.w, ...), custom_call_target="tpu_custom_call" | custom-call | tf_op jit(solution)/shard_map/basis/pallas_call | solution.py:479
Async XLA Ops:
  0.6 0.7 copy-start.6
  0.6 0.7 copy-start.7
  1.3 0.9 copy-start
  2.2 0.9 copy-start.1
  3.1 0.9 copy-start.2
  4.0 0.9 copy-start.3
  4.9 0.8 copy-start.4
  5.8 0.8 copy-start.5

commit v3 on v2

--- a/solution.py
+++ b/solution.py
@@ -45,8 +45,9 @@
 
 def step_kernel(
     tiers, rows,
-    cm, pv, diag, lat, lat_at, vert, vert_at, smo,
-    w_out, early, mid, late,
+    cm_in, pv_in, diag_in, lat_in, lat_at, vert_in, vert_at, smo_in,
+    stacked, early, mid, late,
+    diag, lat, vert, smo, load_sem,
     f_own, f_prev, f_next, f_low, f_up,
     t_prev, t_next, t_low, got_prev, got_next, got_up,
     p_own, p_low, x_own, x_low, wb, wb_prev, wb_next, wb_low, wb_up,
@@ -56,7 +57,13 @@
     count = tiers * rows
     me = tier * rows + row
     bt = diag.shape[-1]
-    k = cm.shape[1]
+    k = cm_in.shape[1]
+    cm, w_out, pv = [stacked.at[:, i * k:(i + 1) * k] for i in range(3)]
+    loads = [
+        pltpu.make_async_copy(source, target, load_sem.at[i]) for i, (source, target) in enumerate(
+            [(cm_in, cm), (pv_in, pv), (lat_in, lat), (vert_in, vert), (diag_in, diag), (smo_in, smo)])]
+    for load in loads:
+        load.start()
 
     def place(d):
         return (lax.div(d, rows), lax.rem(d, rows))
@@ -95,6 +102,8 @@
         def _():
             remote(src, dst, slot, (tier, row)).wait_send()
 
+    for load in loads:
+        load.wait()
     f_own[:, :k] = cm[...].astype(BF16)
     f_own[:, k:] = pv[...].astype(BF16)
     below = flag(lat_at[1, 0] == 0)
@@ -345,10 +354,10 @@
 
 
 def basis_kernel(
-    inverse_rows, early, mid, late, cm, w, pv, ortho, projected, z_ref, a_ref, m_ref
+    inverse_rows, early, mid, late, stacked, ortho, projected, z_ref, a_ref, m_ref
 ):
-    k = cm.shape[1]
-    n = 3 * k
+    n = stacked.shape[1]
+    k = n // 3
 
     def at(ref, i):
         return ref[i * k:(i + 1) * k]
@@ -420,8 +429,7 @@
 
     inverse = z_ref[...] * scale_column
     high, low = halves(inverse)
-    stacked = jnp.concatenate([cm[...], w[...], pv[...]], 1)
-    s_high, s_low = halves(stacked)
+    s_high, s_low = halves(stacked[...])
     ortho[...] = dot(s_high, high) + (dot(s_high, low) + dot(s_low, high))
     half = dot3(inner, inverse)
     projected[...] = dot3(inverse, half, dot_t)
@@ -448,20 +456,22 @@
         for shape in ((n1, k), (n2, k), (n1, k), (2 * tiers, n2, k), (rows // 4, n3, k)):
             boxes.append(pltpu.VMEM(shape, F32))
     smem = pl.BlockSpec(memory_space=pltpu.SMEM)
-    one = pl.BlockSpec(memory_space=pltpu.VMEM)
+    hbm = pl.BlockSpec(memory_space=pltpu.HBM)
     pair = pltpu.VMEM((height, 2 * k), BF16)
     single = pltpu.VMEM((height, k), BF16)
     tall = pltpu.VMEM((height, bt), BF16)
     square = pltpu.VMEM((height, height), BF16)
     wide = pltpu.VMEM((height, k), F32)
-    w, early, mid, late = pl.pallas_call(
+    stacked, early, mid, late = pl.pallas_call(
         functools.partial(step_kernel, tiers, rows),
         out_shape=[
-            jax.ShapeDtypeStruct((height, k), F32)] + [
+            jax.ShapeDtypeStruct((height, 3 * k), F32)] + [
             jax.ShapeDtypeStruct((total, k), F32) for total in totals],
-        in_specs=[one, one, one, one, smem, one, smem, one],
+        in_specs=[hbm, hbm, hbm, hbm, smem, hbm, smem, hbm],
         out_specs=vmem(4),
         scratch_shapes=[
+            pltpu.VMEM((2, bt, bt), BF16), pltpu.VMEM((2, 2, bt, bt), BF16), pltpu.VMEM((2, bt, bt), BF16),
+            pltpu.VMEM((2, bt, bt), F32), pltpu.SemaphoreType.DMA((6,)),
             pair, pair, pair, pair, pair,
             tall, tall, square, tall, tall, square,
             wide, wide, wide, wide, single, single, single, single, single,
@@ -469,7 +479,7 @@
         ] + [pltpu.VMEM((total, k), F32) for total in totals] + [
             pltpu.SemaphoreType.DMA((SEMS,)), pltpu.SemaphoreType.DMA((SEMS,))] + boxes,
         compiler_params=pltpu.CompilerParams(
-            collective_id=0, has_side_effects=True, vmem_limit_bytes=40 * 2**20),
+            collective_id=0, has_side_effects=True, vmem_limit_bytes=60 * 2**20),
         name="step",
     )(
         current_modes, previous, diag_tiles[0, 0], lateral_tiles[0, 0], lateral_index[0, 0],
@@ -479,12 +489,12 @@
     return pl.pallas_call(
         functools.partial(basis_kernel, 1.0 / (height * count)),
         out_shape=[jax.ShapeDtypeStruct((height, n), F32), jax.ShapeDtypeStruct((n, n), F32)],
-        in_specs=vmem(6),
+        in_specs=vmem(4),
         out_specs=vmem(2),
         scratch_shapes=[full, full, full],
-        compiler_params=pltpu.CompilerParams(vmem_limit_bytes=40 * 2**20),
+        compiler_params=pltpu.CompilerParams(vmem_limit_bytes=60 * 2**20),
         name="basis",
-    )(early, mid, late, current_modes, w, previous)
+    )(early, mid, late, stacked)
 
 
 def solution(mesh):

time: 209 us -> 206 us (0.986)
  local copies, waits for them, and re-layouts: 5.96 us -> 0 us
  Pallas kernels: 202 us -> 205 us
    unnamed x16 -> x0, local copies, waits for them, and re-layouts: 5.96 us -> none
where the time goes in v3:
time: 206 us
  Pallas kernels  205 us (100%)
    pallas_call x1, Pallas kernels, on_device(): pl.pallas_call(functools.partial(basis_kernel, 1.0 / (height * count)), o...  159 us
    pallas_call x1, Pallas kernels, on_device(): pl.pallas_call(functools.partial(step_kernel, tiers, rows), out_shape=[ja...  46.6 us

profile of v3, /device:TPU:0, one launch (start us, length us, event | category | flops | bytes accessed | tf_op | source)
XLA Modules:
  0.0 205.7 jit_solution(850239496086847626)
XLA Ops:
  0.6 46.6 %step.1 = (f32[256,384]{1,0:T(8,128)}, f32[768,128]{1,0:T(8,128)}, f32[768,128]{1,0:T(8,128)}, f32[512,128]{1,0:T(8,128)}) custom-call(f32[256,128]{1,0:T(8,128)} %cm_in.1, f32[256,128]{1,0:T(8,128)} %pv_in.1, bf16[2,128,128]{2,1,0:T(8,128)(2,1)} %bitcast.8, bf16[2,2,128,128]{3,2,1,0:T(8,128)(2,1)} %bitcast.6, s32[2,2]{1,0:T(2,128)} %bitcast.10, ...), custom_call_target="tpu_custom_call" | custom-call | tf_op jit(solution)/shard_map/step/pallas_call | solution.py:465
  47.2 158.5 %basis.1 = (f32[256,384]{1,0:T(8,128)}, f32[384,384]{1,0:T(8,128)}) custom-call(f32[768,128]{1,0:T(8,128)} %get-tuple-element.6.early, f32[768,128]{1,0:T(8,128)} %get-tuple-element.7.mid, f32[512,128]{1,0:T(8,128)} %get-tuple-element.8.late, f32[256,384]{1,0:T(8,128)} %get-tuple-element.9.stacked), custom_call_target="tpu_custom_call" | custom-call | tf_op jit(solution)/shard_map/basis/pallas_call | solution.py:489

commit v4 on v3

--- a/solution.py
+++ b/solution.py
@@ -38,8 +38,8 @@
     return (tile.astype(F32) * factor).astype(BF16)
 
 
-F_PREV, F_NEXT, F_LOW, F_UP, T_PREV, T_NEXT, T_LOW, P_UP, W_PREV, W_NEXT, W_LOW, W_UP, QUOT, X_UP = range(14)
-SUM_AT = 14
+F_PREV, F_NEXT, F_LOW, F_UP, T_PREV, T_NEXT, T_LOW, P_UP, W_PREV, W_NEXT, W_LOW, W_UP, QUOT, X_UP, FLAG_LOW = range(15)
+SUM_AT = 15
 SEMS = SUM_AT + 18
 
 
@@ -47,7 +47,7 @@
     tiers, rows,
     cm_in, pv_in, diag_in, lat_in, lat_at, vert_in, vert_at, smo_in,
     stacked, early, mid, late,
-    diag, lat, vert, smo, load_sem,
+    diag, lat, vert, smo, load_sem, swaps, got_swaps, got_vert,
     f_own, f_prev, f_next, f_low, f_up,
     t_prev, t_next, t_low, got_prev, got_next, got_up,
     p_own, p_low, x_own, x_low, wb, wb_prev, wb_next, wb_low, wb_up,
@@ -116,6 +116,7 @@
     t_next[bt:] = lat[1, 1]
     for g in range(2):
         swap = flag(vert_at[g] == 1)
+        swaps[g * 16:(g + 1) * 16] = scaled(jnp.ones((16, bt), BF16), swap)
         t_low[g * bt:(g + 1) * bt, :bt] = scaled(vert[g], 1.0 - swap)
         t_low[g * bt:(g + 1) * bt, bt:] = scaled(vert[g], swap)
 
@@ -147,7 +148,7 @@
     first = [
         (f_own, f_up, F_LOW, LOW), (f_own, f_low, F_UP, UP),
         (f_own, f_next, F_PREV, PREV), (f_own, f_prev, F_NEXT, NEXT),
-        (t_low, got_up, T_LOW, LOW), (t_prev, got_next, T_PREV, PREV), (t_next, got_prev, T_NEXT, NEXT),
+        (vert, got_vert, T_LOW, LOW), (swaps, got_swaps, FLAG_LOW, LOW), (t_prev, got_next, T_PREV, PREV), (t_next, got_prev, T_NEXT, NEXT),
     ]
     second = [
         (wb, wb_up, W_LOW, LOW), (wb, wb_low, W_UP, UP),
@@ -279,6 +280,14 @@
     total = local(f_own[...])
     for item in first:
         receive(*item)
+
+    @pl.when(has_up)
+    def _():
+        for g in range(2):
+            swap = got_swaps[g * 16:(g + 1) * 16].astype(F32)[:1]
+            got_up[g * bt:(g + 1) * bt, :bt] = scaled(got_vert[g], 1.0 - swap)
+            got_up[g * bt:(g + 1) * bt, bt:] = scaled(got_vert[g], swap)
+
     image = coupled(total, f_prev, f_next, f_low, f_up)
     x, mode_image = cm[...], image[:, :k]
     q_buf[pl.ds(me, 1), 0:1] = jnp.sum(x * mode_image, 0, keepdims=True)[None]
@@ -323,25 +332,25 @@
     second_sum.send1()
     first_sum.send2()
     total = local(wb[...])
+    second_sum.send2()
     for item in second:
         receive(*item)
     work_image = coupled(total, wb_prev, wb_next, wb_low, wb_up)
+    second_sum.send3()
+    first_sum.send3()
     product = dot3(jnp.concatenate([fields, w], 1), work_image, dot_t)
     src2[:3 * k] = product
     third_sum.send1()
-    second_sum.send2()
-    first_sum.send3()
+    second_sum.share3()
+    first_sum.share3()
     third_sum.send2()
-    second_sum.send3()
-    first_sum.share3()
+    second_sum.share2()
+    first_sum.share2()
     third_sum.send3()
-    second_sum.share3()
-    first_sum.share2()
+    second_sum.share1()
+    first_sum.share1()
     third_sum.share3()
-    second_sum.share2()
-    first_sum.share1()
     third_sum.share2()
-    second_sum.share1()
     third_sum.share1()
     first_sum.end()
     second_sum.end()
@@ -472,6 +481,7 @@
         scratch_shapes=[
             pltpu.VMEM((2, bt, bt), BF16), pltpu.VMEM((2, 2, bt, bt), BF16), pltpu.VMEM((2, bt, bt), BF16),
             pltpu.VMEM((2, bt, bt), F32), pltpu.SemaphoreType.DMA((6,)),
+            pltpu.VMEM((32, bt), BF16), pltpu.VMEM((32, bt), BF16), pltpu.VMEM((2, bt, bt), BF16),
             pair, pair, pair, pair, pair,
             tall, tall, square, tall, tall, square,
             wide, wide, wide, wide, single, single, single, single, single,

time: 206 us -> 210 us (1.019)
  Pallas kernels: 205 us -> 210 us
    pallas_call x1, Pallas kernels: 46.6 us -> 51.1 us  [on_device(): pl.pallas_call(functools.partial(step_kernel, tiers, rows), out_shape=[ja...]
where the time goes in v4:
time: 210 us
  Pallas kernels  210 us (100%)
    pallas_call x1, Pallas kernels, on_device(): pl.pallas_call(functools.partial(basis_kernel, 1.0 / (height * count)), o...  159 us
    pallas_call x1, Pallas kernels, on_device(): pl.pallas_call(functools.partial(step_kernel, tiers, rows), out_shape=[ja...  51.1 us

profile of v4, /device:TPU:0, one launch (start us, length us, event | category | flops | bytes accessed | tf_op | source)
XLA Modules:
  0.0 210.2 jit_solution(10521513656408132263)
XLA Ops:
  0.6 51.1 %step.1 = (f32[256,384]{1,0:T(8,128)}, f32[768,128]{1,0:T(8,128)}, f32[768,128]{1,0:T(8,128)}, f32[512,128]{1,0:T(8,128)}) custom-call(f32[256,128]{1,0:T(8,128)} %cm_in.1, f32[256,128]{1,0:T(8,128)} %pv_in.1, bf16[2,128,128]{2,1,0:T(8,128)(2,1)} %bitcast.8, bf16[2,2,128,128]{3,2,1,0:T(8,128)(2,1)} %bitcast.6, s32[2,2]{1,0:T(2,128)} %bitcast.10, ...), custom_call_target="tpu_custom_call" | custom-call | tf_op jit(solution)/shard_map/step/pallas_call | solution.py:474
  51.7 158.5 %basis.1 = (f32[256,384]{1,0:T(8,128)}, f32[384,384]{1,0:T(8,128)}) custom-call(f32[768,128]{1,0:T(8,128)} %get-tuple-element.6.early, f32[768,128]{1,0:T(8,128)} %get-tuple-element.7.mid, f32[512,128]{1,0:T(8,128)} %get-tuple-element.8.late, f32[256,384]{1,0:T(8,128)} %get-tuple-element.9.stacked), custom_call_target="tpu_custom_call" | custom-call | tf_op jit(solution)/shard_map/basis/pallas_call | solution.py:499

commit v5 on v3

--- a/solution.py
+++ b/solution.py
@@ -38,8 +38,8 @@
     return (tile.astype(F32) * factor).astype(BF16)
 
 
-F_PREV, F_NEXT, F_LOW, F_UP, T_PREV, T_NEXT, T_LOW, P_UP, W_PREV, W_NEXT, W_LOW, W_UP, QUOT, X_UP = range(14)
-SUM_AT = 14
+F_PREV, F_NEXT, F_LOW, F_UP, T_PREV, T_NEXT, T_LOW, P_UP, W_PREV, W_NEXT, W_LOW, W_UP, QUOT, X_UP, FLAG_LOW = range(15)
+SUM_AT = 15
 SEMS = SUM_AT + 18
 
 
@@ -47,7 +47,7 @@
     tiers, rows,
     cm_in, pv_in, diag_in, lat_in, lat_at, vert_in, vert_at, smo_in,
     stacked, early, mid, late,
-    diag, lat, vert, smo, load_sem,
+    diag, lat, vert, smo, load_sem, swaps, got_swaps, got_vert,
     f_own, f_prev, f_next, f_low, f_up,
     t_prev, t_next, t_low, got_prev, got_next, got_up,
     p_own, p_low, x_own, x_low, wb, wb_prev, wb_next, wb_low, wb_up,
@@ -116,6 +116,7 @@
     t_next[bt:] = lat[1, 1]
     for g in range(2):
         swap = flag(vert_at[g] == 1)
+        swaps[g * 16:(g + 1) * 16] = scaled(jnp.ones((16, bt), BF16), swap)
         t_low[g * bt:(g + 1) * bt, :bt] = scaled(vert[g], 1.0 - swap)
         t_low[g * bt:(g + 1) * bt, bt:] = scaled(vert[g], swap)
 
@@ -147,7 +148,7 @@
     first = [
         (f_own, f_up, F_LOW, LOW), (f_own, f_low, F_UP, UP),
         (f_own, f_next, F_PREV, PREV), (f_own, f_prev, F_NEXT, NEXT),
-        (t_low, got_up, T_LOW, LOW), (t_prev, got_next, T_PREV, PREV), (t_next, got_prev, T_NEXT, NEXT),
+        (vert, got_vert, T_LOW, LOW), (swaps, got_swaps, FLAG_LOW, LOW), (t_prev, got_next, T_PREV, PREV), (t_next, got_prev, T_NEXT, NEXT),
     ]
     second = [
         (wb, wb_up, W_LOW, LOW), (wb, wb_low, W_UP, UP),
@@ -279,6 +280,14 @@
     total = local(f_own[...])
     for item in first:
         receive(*item)
+
+    @pl.when(has_up)
+    def _():
+        for g in range(2):
+            swap = got_swaps[g * 16:(g + 1) * 16].astype(F32)[:1]
+            got_up[g * bt:(g + 1) * bt, :bt] = scaled(got_vert[g], 1.0 - swap)
+            got_up[g * bt:(g + 1) * bt, bt:] = scaled(got_vert[g], swap)
+
     image = coupled(total, f_prev, f_next, f_low, f_up)
     x, mode_image = cm[...], image[:, :k]
     q_buf[pl.ds(me, 1), 0:1] = jnp.sum(x * mode_image, 0, keepdims=True)[None]
@@ -472,6 +481,7 @@
         scratch_shapes=[
             pltpu.VMEM((2, bt, bt), BF16), pltpu.VMEM((2, 2, bt, bt), BF16), pltpu.VMEM((2, bt, bt), BF16),
             pltpu.VMEM((2, bt, bt), F32), pltpu.SemaphoreType.DMA((6,)),
+            pltpu.VMEM((32, bt), BF16), pltpu.VMEM((32, bt), BF16), pltpu.VMEM((2, bt, bt), BF16),
             pair, pair, pair, pair, pair,
             tall, tall, square, tall, tall, square,
             wide, wide, wide, wide, single, single, single, single, single,

time: 206 us -> 205 us (level)
  no operation moved by 1% of the time
where the time goes in v5:
time: 205 us
  Pallas kernels  204 us (100%)
    pallas_call x1, Pallas kernels, on_device(): pl.pallas_call(functools.partial(basis_kernel, 1.0 / (height * count)), o...  159 us
    pallas_call x1, Pallas kernels, on_device(): pl.pallas_call(functools.partial(step_kernel, tiers, rows), out_shape=[ja...  45.7 us

profile of v5, /device:TPU:0, one launch (start us, length us, event | category | flops | bytes accessed | tf_op | source)
XLA Modules:
  0.0 204.8 jit_solution(6490732877660861222)
XLA Ops:
  0.6 45.7 %step.1 = (f32[256,384]{1,0:T(8,128)}, f32[768,128]{1,0:T(8,128)}, f32[768,128]{1,0:T(8,128)}, f32[512,128]{1,0:T(8,128)}) custom-call(f32[256,128]{1,0:T(8,128)} %cm_in.1, f32[256,128]{1,0:T(8,128)} %pv_in.1, bf16[2,128,128]{2,1,0:T(8,128)(2,1)} %bitcast.8, bf16[2,2,128,128]{3,2,1,0:T(8,128)(2,1)} %bitcast.6, s32[2,2]{1,0:T(2,128)} %bitcast.10, ...), custom_call_target="tpu_custom_call" | custom-call | tf_op jit(solution)/shard_map/step/pallas_call | solution.py:474
  46.3 158.5 %basis.1 = (f32[256,384]{1,0:T(8,128)}, f32[384,384]{1,0:T(8,128)}) custom-call(f32[768,128]{1,0:T(8,128)} %get-tuple-element.6.early, f32[768,128]{1,0:T(8,128)} %get-tuple-element.7.mid, f32[512,128]{1,0:T(8,128)} %get-tuple-element.8.late, f32[256,384]{1,0:T(8,128)} %get-tuple-element.9.stacked), custom_call_target="tpu_custom_call" | custom-call | tf_op jit(solution)/shard_map/basis/pallas_call | solution.py:499

commit v6 on v5

--- a/solution.py
+++ b/solution.py
@@ -305,6 +305,15 @@
     smooth(mode_image, p_low, p_own)
     send(p_own, p_low, P_UP, UP)
 
+    everyone = q_buf.at[pl.ds(0, count - 1)]
+    remote(everyone, everyone, QUOT, (tier, row)).wait_recv()
+    sums = jnp.sum(q_buf[...], axis=0)
+    w = p_own[...] - x_own[...] * (sums[0:1] / sums[1:2])
+    w_out[...] = w
+    wb[...] = w.astype(BF16)
+    for item in second:
+        send(*item)
+
     fields = jnp.concatenate([x, pv[...]], 1)
     given = jnp.concatenate([fields, image], 1)
     product = dot3(fields, given, dot_t)
@@ -316,15 +325,6 @@
     src0[5 * k:6 * k] = product[k:, 3 * k:]
     src1[0 * k:1 * k] = product[:k, 3 * k:]
     first_sum.send1()
-
-    everyone = q_buf.at[pl.ds(0, count - 1)]
-    remote(everyone, everyone, QUOT, (tier, row)).wait_recv()
-    sums = jnp.sum(q_buf[...], axis=0)
-    w = p_own[...] - x_own[...] * (sums[0:1] / sums[1:2])
-    w_out[...] = w
-    wb[...] = w.astype(BF16)
-    for item in second:
-        send(*item)
 
     product = dot3(w, jnp.concatenate([given, w], 1), dot_t)
     for at in range(5):

time: 205 us -> 205 us (level)
  no operation moved by 1% of the time
where the time goes in v6:
time: 205 us
  Pallas kernels  204 us (100%)
    pallas_call x1, Pallas kernels, on_device(): pl.pallas_call(functools.partial(basis_kernel, 1.0 / (height * count)), o...  159 us
    pallas_call x1, Pallas kernels, on_device(): pl.pallas_call(functools.partial(step_kernel, tiers, rows), out_shape=[ja...  45.8 us

profile of v6, /device:TPU:0, one launch (start us, length us, event | category | flops | bytes accessed | tf_op | source)
XLA Modules:
  0.0 204.9 jit_solution(13142038900833020702)
XLA Ops:
  0.6 45.8 %step.1 = (f32[256,384]{1,0:T(8,128)}, f32[768,128]{1,0:T(8,128)}, f32[768,128]{1,0:T(8,128)}, f32[512,128]{1,0:T(8,128)}) custom-call(f32[256,128]{1,0:T(8,128)} %cm_in.1, f32[256,128]{1,0:T(8,128)} %pv_in.1, bf16[2,128,128]{2,1,0:T(8,128)(2,1)} %bitcast.8, bf16[2,2,128,128]{3,2,1,0:T(8,128)(2,1)} %bitcast.6, s32[2,2]{1,0:T(2,128)} %bitcast.10, ...), custom_call_target="tpu_custom_call" | custom-call | tf_op jit(solution)/shard_map/step/pallas_call | solution.py:474
  46.4 158.5 %basis.1 = (f32[256,384]{1,0:T(8,128)}, f32[384,384]{1,0:T(8,128)}) custom-call(f32[768,128]{1,0:T(8,128)} %get-tuple-element.6.early, f32[768,128]{1,0:T(8,128)} %get-tuple-element.7.mid, f32[512,128]{1,0:T(8,128)} %get-tuple-element.8.late, f32[256,384]{1,0:T(8,128)} %get-tuple-element.9.stacked), custom_call_target="tpu_custom_call" | custom-call | tf_op jit(solution)/shard_map/basis/pallas_call | solution.py:499
